TPU v7x, 32 devices: a whole 2x2x4 slice. The times are simulated.
32 devices in a mesh: cfg: 2 (over x), sx: 16 (over z, y, core).
Axes of the slice: x: 2, y: 2, z: 4, core: 2. Of those that a mesh axis runs over, the one named last changes fastest.
Arguments:
- eigvecs: bfloat16 [512, 2, 3, 16, 1024], P('cfg', None, None, 'sx'), parts along dimension 0, may hold values from -6 to 6
- link_seed: int32 [6], P('cfg'), parts along dimension 0, may hold values from 1 to 46336
- ownership: int32 [2080], replicated, may hold values from 0 to 2079, each once
Outputs:
- elementals: float32 [4160, 96], P(('cfg', 'sx')), parts along dimension 0
There are 2 independent parts, one for each index of `cfg`. A program takes and returns all parts, laid end to end along the dimension named above; an argument that names none is the same for every part. Nothing has to cross between parts.
Inputs may be any that keep to these rules, and one draw needn't show every extreme that they name: ownership is a permutation of the pair tiles 0 to 2079.
All inputs are finite; a program needn't handle non-finite values.
Results may differ from a plain program's by a relative error of at most 0.0029.
Values may be sent and summed in bfloat16 or wider, within the bound.
No kernel may reach another device: no remote copies, remote signals or barrier semaphores. Data moves between devices by JAX's collectives and lax.ppermute only.
A program may use at most 192 MiB of HBM per device.

v0:
```python
import math

import jax
import jax.numpy as jnp
import numpy as np
from jax import lax
from jax.sharding import PartitionSpec as P

TM = 4
NZ = 64


def from_behind(block, axis, distance):
    devices = range(lax.axis_size(axis))
    route = [((i - distance) % len(devices), i) for i in devices]
    return lax.ppermute(block, axis, route)


def scramble(seed_value, site_code):
    modulus = 46337
    low_part = site_code % modulus
    high_part = site_code // modulus
    mixed_value = (seed_value * seed_value + low_part) % modulus
    mixed_value = (mixed_value * mixed_value + high_part * 977 + 31) % modulus
    angles = []
    for angle_index in range(7):
        scrambled = (mixed_value + 5171 * angle_index + 1) % modulus
        scrambled = (scrambled * scrambled + low_part) % modulus
        scrambled = (scrambled * scrambled + 12345) % modulus
        angles.append(scrambled.astype(jnp.float32) * (2.0 * math.pi / modulus) - math.pi)
    return angles


def link_field(seed_value, site_code):
    angles = scramble(seed_value, site_code)
    cos_alpha, sin_alpha = (jnp.cos(angles[0]), jnp.sin(angles[0]))
    cos_beta, sin_beta = (jnp.cos(angles[1]), jnp.sin(angles[1]))
    cos_gamma, sin_gamma = (jnp.cos(angles[2]), jnp.sin(angles[2]))
    rotation = [
        [
            cos_alpha * cos_beta * cos_gamma - sin_alpha * sin_gamma,
            -cos_alpha * cos_beta * sin_gamma - sin_alpha * cos_gamma,
            cos_alpha * sin_beta,
        ],
        [
            sin_alpha * cos_beta * cos_gamma + cos_alpha * sin_gamma,
            -sin_alpha * cos_beta * sin_gamma + cos_alpha * cos_gamma,
            sin_alpha * sin_beta,
        ],
        [-sin_beta * cos_gamma, sin_beta * sin_gamma, cos_beta],
    ]
    phase_left = [angles[3], angles[4], -angles[3] - angles[4]]
    phase_right = [angles[5], angles[6], -angles[5] - angles[6]]
    link_real = jnp.stack(
        [
            jnp.stack(
                [
                    rotation[row_index][column]
                    * jnp.cos(phase_left[row_index] + phase_right[column])
                    for column in range(3)
                ]
            )
            for row_index in range(3)
        ]
    )
    link_imag = jnp.stack(
        [
            jnp.stack(
                [
                    rotation[row_index][column]
                    * jnp.sin(phase_left[row_index] + phase_right[column])
                    for column in range(3)
                ]
            )
            for row_index in range(3)
        ]
    )
    return (link_real, link_imag)


def hop_vectors(link_real, link_imag, vectors):
    real_part = vectors[:, 0].astype(jnp.float32)
    imag_part = vectors[:, 1].astype(jnp.float32)
    out_real = []
    out_imag = []
    for colour in range(3):
        acc_real = jnp.zeros(real_part[:, 0].shape, jnp.float32)
        acc_imag = jnp.zeros(real_part[:, 0].shape, jnp.float32)
        for source in range(3):
            u_real = link_real[colour, source]
            u_imag = link_imag[colour, source]
            acc_real = acc_real + u_real * real_part[:, source] - u_imag * imag_part[:, source]
            acc_imag = acc_imag + u_real * imag_part[:, source] + u_imag * real_part[:, source]
        out_real.append(acc_real)
        out_imag.append(acc_imag)
    return jnp.stack([jnp.stack(out_real, 1), jnp.stack(out_imag, 1)], 1).astype(jnp.bfloat16)


def shift_along_y(vectors):
    return jnp.roll(vectors, -NZ, 4)


def shift_along_z(vectors):
    plane_sites = vectors.shape[4]
    inside = jnp.roll(vectors, -1, 4)
    wrapped = jnp.roll(vectors, NZ - 1, 4)
    at_edge = jnp.arange(plane_sites, dtype=jnp.int32) % NZ == NZ - 1
    return jnp.where(at_edge, wrapped, inside)


def mode_products(left_side, hopped):
    modes = left_side.shape[0]
    lefts = left_side.reshape(2 * modes, -1)
    rights = hopped.reshape(2 * modes, -1)
    blocks = lax.dot_general(
        lefts, rights, (((1,), (1,)), ((), ())), preferred_element_type=jnp.float32
    )
    blocks = blocks.reshape(modes, 2, modes, 2)
    real_part = blocks[:, 0, :, 0] + blocks[:, 1, :, 1]
    imag_part = blocks[:, 0, :, 1] - blocks[:, 1, :, 0]
    return jnp.stack([real_part, imag_part], 0)


def tile_table(products):
    modes = products.shape[2]
    tile_count = modes // TM
    tiles = products.reshape(3, 2, tile_count, TM, tile_count, TM).transpose(2, 4, 0, 1, 3, 5)
    return tiles.reshape(tile_count * tile_count, 6 * TM * TM)


def per_device(eigvecs, link_seed, ownership):
    modes, _, _, layers, plane_sites = eigvecs.shape
    extent_x = layers * lax.axis_size("sx")
    device_index = lax.axis_index("sx")
    global_x = device_index * layers + jnp.arange(layers, dtype=jnp.int32)
    plane_index = jnp.arange(plane_sites, dtype=jnp.int32)
    site_code = global_x[:, None] * plane_sites + plane_index[None, :]
    hop_y = hop_vectors(*link_field(link_seed[1], site_code), shift_along_y(eigvecs))
    hop_z = hop_vectors(*link_field(link_seed[2], site_code), shift_along_z(eigvecs))
    product_y = mode_products(eigvecs, hop_y)
    product_z = mode_products(eigvecs, hop_z)
    upper_face = from_behind(eigvecs, "sx", -1)
    nearest = jnp.concatenate([eigvecs[:, :, :, 1:], upper_face], 3)
    hop_x = hop_vectors(*link_field(link_seed[0], site_code), nearest)
    product_x = mode_products(eigvecs, hop_x)
    products = jnp.stack([product_x, product_y, product_z], 0)
    tile_count = modes // TM
    upper_rows, upper_cols = np.triu_indices(tile_count)
    pair_rows = jnp.asarray((upper_rows * tile_count + upper_cols).astype(np.int32))
    mirror_rows = jnp.asarray((upper_cols * tile_count + upper_rows).astype(np.int32))
    chosen_rows = jnp.take(pair_rows, ownership)
    normalise = 1.0 / math.sqrt(12.0 * extent_x * plane_sites)
    entries = 6 * TM * TM
    chosen_mirror = jnp.take(mirror_rows, ownership)
    both_rows = jnp.stack([chosen_rows, chosen_mirror], 1)
    packed = jnp.take(tile_table(products), both_rows, axis=0).reshape(-1, 2 * entries)
    summed = lax.psum_scatter(packed, "sx", scatter_dimension=0, tiled=True)
    direct = summed[:, :entries].reshape(-1, 3, 2, TM, TM)
    mirror = jnp.swapaxes(summed[:, entries:].reshape(-1, 3, 2, TM, TM), 3, 4)
    real_part = direct[:, :, 0] - mirror[:, :, 0]
    imag_part = direct[:, :, 1] + mirror[:, :, 1]
    return jnp.stack([real_part, imag_part], 2).reshape(-1, entries) * normalise


def solution(mesh):
    return jax.shard_map(
        per_device,
        mesh=mesh,
        in_specs=(P("cfg", None, None, "sx", None), P("cfg"), P()),
        out_specs=P(("cfg", "sx"), None),
        check_vma=False,
    )
```

profile of v0, /device:TPU:0, one launch (start us, length us, event | category | flops | bytes accessed | tf_op | source)
XLA Modules:
  0.0 703.8 jit_solution(16824374799865171374)
XLA Ops:
  6.5 4.6 copy.71
  11.1 5.4 collective-permute-start
  48.9 3.7 slice.587
  52.6 5.6 slice.553
  58.2 4.3 copy.73
  62.9 11.4 %gather_fusion.2 = s32[2080]{0:T(1024)S(1)} fusion(s32[2080]{0:T(1024)S(1)} %copy-done.1, s32[3072]{0:T(1024)S(1)} %pad_clamp_fusion.1), kind=kCustom, calls=%fused_computation.1.clone | custom fusion | bytes 24960 | tf_op jit(solution)/shard_map/jit(_take)/gather | solution.py:154
  74.3 11.4 %gather_fusion.1 = s32[2080]{0:T(1024)S(1)} fusion(s32[2080]{0:T(1024)S(1)} %copy-done, s32[3072]{0:T(1024)S(1)} %pad_clamp_fusion.1), kind=kCustom, calls=%fused_computation.clone | custom fusion | bytes 24960 | tf_op jit(solution)/shard_map/jit(_take)/gather | solution.py:151
  87.0 2.8 fusion.8
  93.1 2.7 copy.79
  97.6 4.4 maximum_select_fusion
  117.7 68.4 %reshape.5098 = f32[256,2,256,2]{3,2,1,0:T(8,128)} reshape(f32[512,512]{1,0:T(8,128)S(1)} %copy.88) | data formatting | bytes 2097152 | tf_op jit(solution)/shard_map/reshape | solution.py:118
  186.1 46.5 %fusion.1 = (f32[256,256]{1,0:T(8,128)S(1)}, f32[256,256]{1,0:T(8,128)S(1)}) fusion(f32[256,2,256,2]{3,2,1,0:T(8,128)} %reshape.5098), kind=kLoop, calls=%fused_computation.6 | loop fusion | flops 131072 | bytes 1572864 | tf_op jit(solution)/shard_map/add | solution.py:119
  232.6 68.4 %reshape.5097 = f32[256,2,256,2]{3,2,1,0:T(8,128)} reshape(f32[512,512]{1,0:T(8,128)S(1)} %copy.80) | data formatting | bytes 2097152 | tf_op jit(solution)/shard_map/reshape | solution.py:118
  301.0 46.7 %fusion.3 = (f32[256,256]{1,0:T(8,128)S(1)}, f32[256,256]{1,0:T(8,128)S(1)}) fusion(f32[256,2,256,2]{3,2,1,0:T(8,128)} %reshape.5097), kind=kLoop, calls=%fused_computation.10 | loop fusion | flops 131072 | bytes 1572864 | tf_op jit(solution)/shard_map/add | solution.py:119
  349.6 10.1 %add.14181 = f32[1,1,64,4,64,4]{5,4,3,2,1,0:T(8,128)} reshape(f32[256,256]{1,0:T(8,128)S(1)} %get-tuple-element.10) | data formatting | bytes 524288 | tf_op jit(solution)/shard_map/add | solution.py:119
  359.6 6.1 copy.89
  365.8 10.0 %sub.671 = f32[1,1,64,4,64,4]{5,4,3,2,1,0:T(8,128)} reshape(f32[256,256]{1,0:T(8,128)S(1)} %get-tuple-element.11) | data formatting | bytes 524288 | tf_op jit(solution)/shard_map/sub | solution.py:120
  375.8 6.1 copy.90
  381.9 10.0 %add.14098 = f32[1,1,64,4,64,4]{5,4,3,2,1,0:T(8,128)} reshape(f32[256,256]{1,0:T(8,128)S(1)} %get-tuple-element.8) | data formatting | bytes 524288 | tf_op jit(solution)/shard_map/add | solution.py:119
  392.0 6.1 copy.81
  398.1 10.0 %sub.649 = f32[1,1,64,4,64,4]{5,4,3,2,1,0:T(8,128)} reshape(f32[256,256]{1,0:T(8,128)S(1)} %get-tuple-element.9) | data formatting | bytes 524288 | tf_op jit(solution)/shard_map/sub | solution.py:120
  408.2 6.3 copy.82
  427.2 3.1 copy.72
  434.4 68.4 %reshape.5096 = f32[256,2,256,2]{3,2,1,0:T(8,128)} reshape(f32[512,512]{1,0:T(8,128)S(1)} %copy.74) | data formatting | bytes 2097152 | tf_op jit(solution)/shard_map/reshape | solution.py:118
  502.7 46.5 %fusion.5 = (f32[256,256]{1,0:T(8,128)S(1)}, f32[256,256]{1,0:T(8,128)S(1)}) fusion(f32[256,2,256,2]{3,2,1,0:T(8,128)} %reshape.5096), kind=kLoop, calls=%fused_computation.14 | loop fusion | flops 131072 | bytes 1572864 | tf_op jit(solution)/shard_map/add | solution.py:119
  549.3 10.1 %add.14016 = f32[1,1,64,4,64,4]{5,4,3,2,1,0:T(8,128)} reshape(f32[256,256]{1,0:T(8,128)S(1)} %get-tuple-element.6) | data formatting | bytes 524288 | tf_op jit(solution)/shard_map/add | solution.py:119
  559.3 6.3 copy.75
  565.6 10.0 %sub.627 = f32[1,1,64,4,64,4]{5,4,3,2,1,0:T(8,128)} reshape(f32[256,256]{1,0:T(8,128)S(1)} %get-tuple-element.7) | data formatting | bytes 524288 | tf_op jit(solution)/shard_map/sub | solution.py:120
  575.7 6.1 copy.76
  587.8 8.7 %gather_fusion = f32[4160,96]{1,0:T(8,128)} fusion(f32[4096,96]{1,0:T(8,128)S(1)} %copy.92, s32[5120]{0:T(1024)S(1)} %pad_clamp_fusion), kind=kCustom, calls=%fused_computation.2 | custom fusion | bytes 3211520 | tf_op jit(solution)/shard_map/jit(_take)/gather | solution.py:156
  596.5 3.0 copy.93
  602.2 92.5 %all-reduce.3.cloned.1.call-done = f32[2080,192]{0,1:T(8,128)} async-done(((f32[2080,192]{0,1:T(8,128)}), f32[2080,192]{0,1:T(8,128)}) %all-reduce.3.cloned.1.call-update) | async-done | bytes 1597456
  (168 shorter events, 78.9 us)
Async XLA Ops:
  6.5 10.0 %copy-start.14 = (s32[3]{0:T(128)S(1)}, s32[3]{0:T(128)}, u32[]{:S(2)}) copy-start(s32[3]{0:T(128)} %param.8) | copy-start | bytes 40
  6.5 688.1 %all-reduce.3.cloned.1.call-start = ((), (), s32[]{:S(2)}) async-start(), calls=%async_computation | async-start | bytes 3342336
  11.1 410.2 %collective-permute-start = (bf16[256,2,3,1,1024]{4,0,2,3,1:T(8,128)(2,1)}, bf16[256,2,3,1,1024]{4,0,2,3,1:T(8,128)(2,1)}, u32[]{:S(2)}, u32[]{:S(2)}) collective-permute-start(bf16[256,2,3,1,1024]{4,0,2,3,1:T(8,128)(2,1)} %copy.71), channel_id=1, source_target_pairs={{1,0},{2,1},{3,2},{4,3},{5,4},{6,5},{7,6},{8,7},{9,8},{10,9},{11,1... | collective-permute-start | bytes 9437192 | tf_op jit(solution)/shard_map/ppermute | solution.py:16
  52.5 5.7 copy-start.3
  58.2 4.7 copy-start.13
  58.2 4.7 copy-start.1
  62.9 11.4 %copy-start = (s32[2080]{0:T(1024)S(1)}, s32[2080]{0:T(1024)}, u32[]{:S(2)}) copy-start(s32[2080]{0:T(1024)} %constant.353.clone2.1) | copy-start | bytes 24964
  85.8 0.6 copy-start.10
  85.8 0.6 copy-start.8
  95.8 1.8 copy-start.6
  95.8 1.8 copy-start.7
  108.7 2.2 copy-start.2
  112.7 2.0 copy-start.4
  301.0 47.7 %copy-start.9 = (s32[2080]{0:T(1024)S(1)}, s32[2080]{0:T(1024)}, u32[]{:S(2)}) copy-start(s32[2080]{0:T(1024)} %copy-done.8) | copy-start | bytes 24964
  301.0 47.7 %copy-start.11 = (s32[2080]{0:T(1024)S(1)}, s32[2080]{0:T(1024)}, u32[]{:S(2)}) copy-start(s32[2080]{0:T(1024)} %copy-done.10) | copy-start | bytes 24964
  301.0 47.7 %copy-start.12 = (s32[2080,2,1]{0,2,1:T(1,128)S(1)}, s32[2080,2,1]{0,2,1:T(1,128)}, u32[]{:S(2)}) copy-start(s32[2080,2,1]{0,2,1:T(1,128)} %compare_select_fusion) | copy-start | bytes 49924
  408.2 12.9 %copy-start.16 = (f32[1,1,1024]{2,1,0:T(1,128)S(1)}, f32[1,1,1024]{2,1,0:T(1,128)}, u32[]{:S(2)}) copy-start(f32[1,1,1024]{2,1,0:T(1,128)} %get-tuple-element.139) | copy-start | bytes 12292
  408.2 12.9 %copy-start.17 = (f32[1,1,1024]{2,1,0:T(1,128)S(1)}, f32[1,1,1024]{2,1,0:T(1,128)}, u32[]{:S(2)}) copy-start(f32[1,1,1024]{2,1,0:T(1,128)} %get-tuple-element.140) | copy-start | bytes 12292
  408.2 12.9 %copy-start.18 = (f32[1,1,1024]{2,1,0:T(1,128)S(1)}, f32[1,1,1024]{2,1,0:T(1,128)}, u32[]{:S(2)}) copy-start(f32[1,1,1024]{2,1,0:T(1,128)} %get-tuple-element.138) | copy-start | bytes 12292
  408.2 12.9 %copy-start.15 = (f32[1,1,1024]{2,1,0:T(1,128)S(1)}, f32[1,1,1024]{2,1,0:T(1,128)}, u32[]{:S(2)}) copy-start(f32[1,1,1024]{2,1,0:T(1,128)} %get-tuple-element.137) | copy-start | bytes 12292
  430.3 1.9 copy-start.5
  599.5 1.4 copy-start.19
Sparse Core Ops, SparseCore 0:
  601.0 93.5 all-reduce.2
where the time goes:
time: 714 us; the launch traced here: 704 us
  local copies, waits for them, and re-layouts  386 us (54%)
  other arithmetic  194 us (27%)
  waiting for transfers between devices  92.5 us (13%)
  between operations  19 us (3%)
    reshape x3, local copies, waits for them, and re-layouts, mode_products(): blocks = blocks.reshape(modes, 2, modes, 2)  205 us
    add x3, other arithmetic, mode_products(): real_part = blocks[:, 0, :, 0] + blocks[:, 1, :, 1]  140 us
    unnamed x2, waiting for transfers between devices  92.5 us
    sub x6, local copies, waits for them, and re-layouts, mode_products(): imag_part = blocks[:, 0, :, 1] - blocks[:, 1, :, 0]  48.7 us
    add x6, local copies, waits for them, and re-layouts, mode_products(): real_part = blocks[:, 0, :, 0] + blocks[:, 1, :, 1]  48.7 us
    mul x27, other arithmetic, link_field(): rotation[row_index][column]  29.8 us
    unnamed x48, local copies, waits for them, and re-layouts  17.6 us
  transfers between devices with their start and end apart: 2, of which 1 were waited for; matrix products, arithmetic and copies ran while one was open for 57% of the time, Pallas kernels for 0%

commit v1 on v0

v1 whole, which is shorter than its diff:
```python
import functools
import math

import jax
import jax.numpy as jnp
from jax import lax
from jax.experimental import pallas as pl
from jax.experimental.pallas import tpu as pltpu
from jax.sharding import PartitionSpec as P

TM = 4
NZ = 64
LANES = 128
MODULUS = 46337
CHUNKS = 4
F32 = jnp.float32
BF16 = jnp.bfloat16
NT = (((1,), (1,)), ((), ()))


def dot(left, right, dims=(((1,), (0,)), ((), ()))):
    return lax.dot_general(left, right, dims, preferred_element_type=F32)


def iota(shape, axis):
    return lax.broadcasted_iota(jnp.int32, shape, axis)


def round_up(value, step):
    return -(-value // step) * step


def link_angles(seed, site):
    low = lax.rem(site, MODULUS)
    high = lax.div(site, MODULUS)
    mixed = lax.rem(seed * seed + low, MODULUS)
    mixed = lax.rem(mixed * mixed + high * 977 + 31, MODULUS)
    angles = []
    for index in range(7):
        g = lax.rem(mixed + (5171 * index + 1), MODULUS)
        g = lax.rem(g * g + low, MODULUS)
        g = lax.rem(g * g + 12345, MODULUS)
        angles.append(g.astype(F32) * (2.0 * math.pi / MODULUS) - math.pi)
    return angles


def store_links(u_ref, seed, site):
    a = link_angles(seed, site)
    ca, sa = jnp.cos(a[0]), jnp.sin(a[0])
    cb, sb = jnp.cos(a[1]), jnp.sin(a[1])
    cg, sg = jnp.cos(a[2]), jnp.sin(a[2])
    rotation = [
        [ca * cb * cg - sa * sg, -ca * cb * sg - sa * cg, ca * sb],
        [sa * cb * cg + ca * sg, -sa * cb * sg + ca * cg, sa * sb],
        [-sb * cg, sb * sg, cb],
    ]
    left = [a[3], a[4], -a[3] - a[4]]
    right = [a[5], a[6], -a[5] - a[6]]
    for c in range(3):
        for s in range(3):
            phase = left[c] + right[s]
            u_ref[2 * (3 * c + s)] = rotation[c][s] * jnp.cos(phase)
            u_ref[2 * (3 * c + s) + 1] = rotation[c][s] * jnp.sin(phase)


def hop(load, out_ref, u_ref, modes, plane, shift):
    tiles = plane // LANES
    for t in range(tiles):

        def body(block, carry, t=t):
            rows = pl.ds(pl.multiple_of(block * 16, 16), 16)
            lane = iota((16, LANES), 1)
            v = []
            for source in range(3):
                for part in range(2):
                    x = load(part, source, rows, t).astype(F32)
                    if shift == "y":
                        above = load(part, source, rows, (t + 1) % tiles).astype(F32)
                        x = pltpu.roll(jnp.where(lane < NZ, above, x), NZ, 1)
                    elif shift == "z":
                        inside = pltpu.roll(x, LANES - 1, 1)
                        wrapped = pltpu.roll(x, NZ - 1, 1)
                        x = jnp.where(lane % NZ == NZ - 1, wrapped, inside)
                    v.append(x)
            for c in range(3):
                real = imag = None
                for s in range(3):
                    ur = u_ref[2 * (3 * c + s), t : t + 1, :]
                    ui = u_ref[2 * (3 * c + s) + 1, t : t + 1, :]
                    re, im = v[2 * s], v[2 * s + 1]
                    real = ur * re if real is None else real + ur * re
                    real = real - ui * im
                    imag = ur * im if imag is None else imag + ur * im
                    imag = imag + ui * re
                lanes = slice(c * plane + t * LANES, c * plane + (t + 1) * LANES)
                out_ref[rows, lanes] = real.astype(BF16)
                low = pl.ds(pl.multiple_of(modes + block * 16, 16), 16)
                out_ref[low, lanes] = imag.astype(BF16)
            return carry

        lax.fori_loop(0, modes // 16, body, 0)


def products(hop_ref, left_ref, modes, all_modes):
    by_real = dot(hop_ref[...], left_ref[:all_modes, :], NT)
    by_imag = dot(hop_ref[...], left_ref[all_modes:, :], NT)
    real = by_real[:modes] + by_imag[modes:]
    imag = by_real[modes:] - by_imag[:modes]
    return real, imag


class Slots:
    def __init__(self, all_modes, slots, directions):
        self.tiles = all_modes // TM
        assert 2 * self.tiles == LANES
        self.half = self.tiles // 2
        self.depth = round_up((self.half + 1) * self.tiles, 2 * LANES)
        self.columns = 2 * TM * TM * directions
        self.groups = LANES // self.columns
        self.per_group = -(-slots // self.groups)
        self.rows = round_up(self.per_group, 8)
        self.sent = round_up(self.rows, 16)

    def arrange(self, ownership, devices):
        slots = ownership.shape[0] // devices
        spread = jnp.pad(
            ownership.reshape(devices, slots),
            ((0, 0), (0, self.groups * self.per_group - slots)),
            constant_values=-1,
        ).reshape(devices, self.groups, self.per_group)
        spread = jnp.pad(
            spread, ((0, 0), (0, 0), (0, self.rows - self.per_group)), constant_values=-1
        )
        return spread.reshape(devices, self.groups * self.rows, 1)

    def codes(self):
        lane = iota((1, self.depth), 1)
        first, second = lane // self.tiles, lane % self.tiles
        last = self.tiles - 1
        diagonal = first == self.half
        turned = jnp.logical_or(diagonal, second < first)
        i = jnp.where(diagonal, last - second, jnp.where(turned, last - first, first))
        j = jnp.where(turned, last - second, second)
        pair = i * self.tiles - (i * (i - 1)) // 2 + (j - i)
        known = jnp.logical_and(
            first <= self.half, jnp.logical_not(jnp.logical_and(diagonal, second >= self.half))
        )
        return jnp.where(known, pair, -2)


def store_table(table_ref, fold_ref, base, real, imag, slots):
    all_modes = real.shape[0]
    n, half = slots.tiles, slots.half
    parts = [real.T - real, imag.T + imag]

    def choose(count, width, turned):
        row, column = iota((count, all_modes), 0), iota((count, all_modes), 1)
        r, i = row // width, row % width
        if turned:
            i = n - 1 - i
        return (column == i * TM + r).astype(F32).astype(BF16)

    pick = [choose(TM * half, half, turned) for turned in (False, True)]
    spread = [choose(all_modes, n, turned) for turned in (False, True)]
    row_i = iota((TM * half, all_modes), 0) % half
    lane_j = iota((TM * half, all_modes), 1) % n
    corners = []
    for part in range(2):
        entries = parts[part].astype(BF16)
        straight, turned = [
            dot(dot(pick[k], entries).astype(BF16), spread[k], NT) for k in range(2)
        ]
        folded = jnp.where(lane_j >= row_i, straight, turned)
        for k in range(TM // 2):
            fold_ref[k, part * TM * half : (part + 1) * TM * half, :] = folded[
                :, k * LANES : (k + 1) * LANES
            ]
        diagonal = jnp.where(lane_j == row_i, turned, 0.0)
        for r in range(TM):
            corners.append(
                jnp.sum(diagonal[r * half : (r + 1) * half], axis=0, keepdims=True)
            )
    low = iota((2 * TM, LANES), 1) < n

    def split(even, odd, lanes):
        for pair in range(TM // 2):
            e, o = even[pair], odd[pair]
            top = base + 2 * pair * 2 * TM
            table_ref[top : top + 2 * TM, lanes] = jnp.where(low, e, pltpu.roll(o, n, 1))
            table_ref[top + 2 * TM : top + 4 * TM, lanes] = jnp.where(
                low, pltpu.roll(e, n, 1), o
            )

    halves = [slice(k * LANES, (k + 1) * LANES) for k in range(TM // 2)]
    for two in range(half // 2):
        even = [fold_ref[k, pl.ds(2 * two, 2 * TM, stride=half), :] for k in range(TM // 2)]
        odd = [fold_ref[k, pl.ds(2 * two + 1, 2 * TM, stride=half), :] for k in range(TM // 2)]
        split(even, odd, slice(two * LANES, (two + 1) * LANES))
    corner = jnp.concatenate(corners, 0)
    nothing = jnp.zeros((2 * TM, LANES), F32)
    start = half * n
    split([corner[:, h] for h in halves], [nothing] * len(halves), slice(start, start + LANES))
    rest = slots.depth - start - LANES
    if rest:
        table_ref[base : base + 2 * TM * TM, start + LANES :] = jnp.zeros(
            (2 * TM * TM, rest), F32
        )


def send_tiles(out_ref, owner_ref, table_ref, slots, directions):
    block = 2 * TM * TM
    row, column = iota((LANES, slots.columns), 0), iota((LANES, slots.columns), 1)
    entry = row % slots.columns
    direction, inside = entry // block, entry % block
    u = inside % TM
    part_r = inside // TM
    order = column == direction * block + u * (2 * TM) + part_r
    table = dot(order.astype(F32).astype(BF16), table_ref[...].astype(BF16)).astype(BF16)
    codes = slots.codes()
    lane_group = iota((slots.rows, LANES), 1) // slots.columns

    def body(device, carry):
        owners = owner_ref[device]
        chosen = (owners == codes).astype(F32).astype(BF16)
        picked = dot(chosen, table, NT)
        packed = picked[: slots.rows]
        for group in range(1, slots.groups):
            piece = picked[group * slots.rows : (group + 1) * slots.rows]
            packed = jnp.where(lane_group == group, piece, packed)
        if slots.sent > slots.rows:
            packed = jnp.concatenate(
                [packed, jnp.zeros((slots.sent - slots.rows, LANES), F32)], 0
            )
        out_ref[device] = packed.astype(BF16)
        return carry

    lax.fori_loop(0, out_ref.shape[0], body, 0)


def inner_kernel(
    slots, seed_ref, where_ref, owner_ref, *refs
):
    vectors = refs[:CHUNKS]
    sent_ref, left_ref, links_x_ref, hop_ref, u_ref, table_ref, fold_ref = refs[CHUNKS:]
    _, _, part_modes, plane = vectors[0].shape
    all_modes = part_modes * CHUNKS
    for q in range(CHUNKS):
        for c in range(3):
            for part in range(2):
                left_ref[
                    part * all_modes + q * part_modes : part * all_modes + (q + 1) * part_modes,
                    c * plane : (c + 1) * plane,
                ] = vectors[q][c, part]
    tiles = plane // LANES
    site = iota((tiles, LANES), 0) * LANES + iota((tiles, LANES), 1) + where_ref[0] * plane
    store_links(links_x_ref, seed_ref[0], site)

    def load(part, colour, rows, t):
        return left_ref[
            pl.ds(pl.multiple_of(part * all_modes + rows.start, 16), 16),
            colour * plane + t * LANES : colour * plane + (t + 1) * LANES,
        ]

    for d, shift in ((1, "y"), (2, "z")):
        store_links(u_ref, seed_ref[d], site)
        hop(load, hop_ref, u_ref, all_modes, plane, shift)
        real, imag = products(hop_ref, left_ref, all_modes, all_modes)
        store_table(table_ref, fold_ref, (d - 1) * 2 * TM * TM, real, imag, slots)
    send_tiles(sent_ref, owner_ref, table_ref, slots, 2)


def hop_received(vector_ref, links_ref, left_hbm, left_ref, hop_ref, sem):
    copy = pltpu.make_async_copy(left_hbm, left_ref, sem)
    copy.start()
    _, _, modes, plane = vector_ref.shape

    def load(part, colour, rows, t):
        return vector_ref[colour, part, rows, t * LANES : (t + 1) * LANES]

    hop(load, hop_ref, links_ref, modes, plane, None)
    copy.wait()
    return products(hop_ref, left_ref, modes, left_ref.shape[0] // 2)


def outer_kernel(vector_ref, links_ref, left_hbm, out_ref, left_ref, hop_ref, sem):
    real, imag = hop_received(vector_ref, links_ref, left_hbm, left_ref, hop_ref, sem)
    out_ref[0] = real
    out_ref[1] = imag


def last_kernel(slots, owner_ref, *refs):
    before = refs[: CHUNKS - 1]
    (vector_ref, links_ref, left_hbm, sent_ref, left_ref, hop_ref, sem, table_ref, fold_ref) = refs[
        CHUNKS - 1 :
    ]
    real, imag = hop_received(vector_ref, links_ref, left_hbm, left_ref, hop_ref, sem)
    real = jnp.concatenate([b[0] for b in before] + [real], 0)
    imag = jnp.concatenate([b[1] for b in before] + [imag], 0)
    store_table(table_ref, fold_ref, 0, real, imag, slots)
    send_tiles(sent_ref, owner_ref, table_ref, slots, 1)


def finish_kernel(normalise, slots_x, slots_yz, x_ref, yz_ref, out_ref):
    here = out_ref.shape[0]
    start = 0
    for slots, ref in ((slots_x, x_ref), (slots_yz, yz_ref)):
        total = ref[0].astype(F32)
        for device in range(1, ref.shape[0]):
            total = total + ref[device].astype(F32)
        total = total * normalise
        for group in range(slots.groups):
            first = group * slots.per_group
            count = min(slots.per_group, here - first)
            out_ref[first : first + count, start : start + slots.columns] = total[
                :count, group * slots.columns : (group + 1) * slots.columns
            ]
        start += slots.columns


def params(mib):
    return pltpu.CompilerParams(vmem_limit_bytes=mib * 1024 * 1024)


def cost(flops, moved):
    return pl.CostEstimate(flops=flops, bytes_accessed=moved, transcendentals=0)


def per_device(eigvecs, link_seed, ownership):
    modes, _, _, layers, plane = eigvecs.shape
    assert layers == 1
    devices = lax.axis_size("sx")
    here = ownership.shape[0] // devices
    part_modes = modes // CHUNKS
    depth = 3 * plane
    tiles = plane // LANES
    slots_x = Slots(modes, here, 1)
    slots_yz = Slots(modes, here, 2)
    vmem = pl.BlockSpec(memory_space=pltpu.VMEM)
    smem = pl.BlockSpec(memory_space=pltpu.SMEM)
    anywhere = pl.BlockSpec(memory_space=pl.ANY)

    route = [(i, (i - 1) % devices) for i in range(devices)]
    own, upper = [], []
    for q in range(CHUNKS):
        piece = eigvecs[q * part_modes : (q + 1) * part_modes, :, :, 0]
        piece = piece.transpose(2, 1, 0, 3)
        own.append(piece)
        upper.append(lax.ppermute(piece, "sx", route))

    where = lax.axis_index("sx").reshape(1).astype(jnp.int32)
    flops = 4 * modes * modes * depth * 2

    sent_yz, left, links_x = pl.pallas_call(
        functools.partial(inner_kernel, slots_yz),
        name="inner_directions",
        out_shape=(
            jax.ShapeDtypeStruct((devices, slots_yz.sent, LANES), BF16),
            jax.ShapeDtypeStruct((2 * modes, depth), BF16),
            jax.ShapeDtypeStruct((18, tiles, LANES), F32),
        ),
        in_specs=[smem, smem, vmem] + [vmem] * CHUNKS,
        out_specs=(vmem, vmem, vmem),
        scratch_shapes=[
            pltpu.VMEM((2 * modes, depth), BF16),
            pltpu.VMEM((18, tiles, LANES), F32),
            pltpu.VMEM((slots_yz.columns, slots_yz.depth), F32),
            pltpu.VMEM((TM // 2, modes, LANES), F32),
        ],
        compiler_params=params(48),
        cost_estimate=cost(4 * flops, 12 * 2**20),
    )(link_seed, where, slots_yz.arrange(ownership, devices), *own)

    received_yz = lax.all_to_all(sent_yz, "sx", 0, 0)

    scratch = [
        pltpu.VMEM((2 * modes, depth), BF16),
        pltpu.VMEM((2 * part_modes, depth), BF16),
        pltpu.SemaphoreType.DMA,
    ]
    partial = [
        pl.pallas_call(
            outer_kernel,
            name="outer_direction",
            out_shape=jax.ShapeDtypeStruct((2, part_modes, modes), F32),
            in_specs=[vmem, vmem, anywhere],
            out_specs=vmem,
            scratch_shapes=scratch,
            compiler_params=params(32),
            cost_estimate=cost(flops // CHUNKS, 4 * 2**20),
        )(upper[q], links_x, left)
        for q in range(CHUNKS - 1)
    ]
    sent_x = pl.pallas_call(
        functools.partial(last_kernel, slots_x),
        name="outer_direction_tiles",
        out_shape=jax.ShapeDtypeStruct((devices, slots_x.sent, LANES), BF16),
        in_specs=[vmem] + [vmem] * (CHUNKS - 1) + [vmem, vmem, anywhere],
        out_specs=vmem,
        scratch_shapes=scratch
        + [
            pltpu.VMEM((slots_x.columns, slots_x.depth), F32),
            pltpu.VMEM((TM // 2, modes, LANES), F32),
        ],
        compiler_params=params(48),
        cost_estimate=cost(flops, 8 * 2**20),
    )(slots_x.arrange(ownership, devices), *partial, upper[-1], links_x, left)
    received_x = lax.all_to_all(sent_x, "sx", 0, 0)

    extent_x = layers * devices
    normalise = 1.0 / math.sqrt(12.0 * extent_x * plane)
    return pl.pallas_call(
        functools.partial(finish_kernel, normalise, slots_x, slots_yz),
        name="sum_of_devices",
        out_shape=jax.ShapeDtypeStruct((here, slots_x.columns + slots_yz.columns), F32),
        in_specs=[vmem, vmem],
        out_specs=vmem,
        compiler_params=params(32),
    )(received_x, received_yz)


def solution(mesh):
    return jax.shard_map(
        per_device,
        mesh=mesh,
        in_specs=(P("cfg", None, None, "sx", None), P("cfg"), P()),
        out_specs=P(("cfg", "sx"), None),
        check_vma=False,
    )
```

time: 714 us -> 103 us (0.14); the launches traced: 704 us -> 102 us
  local copies, waits for them, and re-layouts: 386 us -> 9.21 us
  other arithmetic: 194 us -> 0 us
  waiting for transfers between devices: 92.5 us -> 0.01 us
  Pallas kernels: 0 us -> 67.8 us
  between operations: 19 us -> 0.2 us
  blocking collectives: 0 us -> 14.6 us
    reshape x8 -> x5, local copies, waits for them, and re-layouts: 209 us -> 1.08 us  [the longest x2 0.79 us: arrange(): return spread.reshape(devices, self.groups * self.rows, 1)]
    add x3 -> x0, other arithmetic: 140 us -> none  [mode_products(): real_part = blocks[:, 0, :, 0] + blocks[:, 1, :, 1]]
    unnamed x2 -> x0, waiting for transfers between devices: 92.5 us -> none
    pallas_call x0 -> x6, Pallas kernels: none -> 67.8 us  [the longest x1 44.8 us: per_device(): pl.pallas_call(functools.partial(inner_kernel, slots_yz), name='inner_dir...]
    sub x6 -> x0, local copies, waits for them, and re-layouts: 48.7 us -> none  [mode_products(): imag_part = blocks[:, 0, :, 1] - blocks[:, 1, :, 0]]
    add x6 -> x0, local copies, waits for them, and re-layouts: 48.7 us -> none  [mode_products(): real_part = blocks[:, 0, :, 0] + blocks[:, 1, :, 1]]
    gather x4 -> x0, local copies, waits for them, and re-layouts: 34.6 us -> none  [the longest x2 11.7 us: per_device(): jnp.take(tile_table(products), both_rows, axis=0).reshape(-1, 2 * entries)]
    mul x28 -> x0, other arithmetic: 29.9 us -> none  [the longest x27 29.8 us: link_field(): rotation[row_index][column]]
  transfers between devices with their start and end apart: 2 -> 5, of which waited for: 1 -> 0; matrix products, arithmetic and copies ran while one was open for 57% -> 3% of each run, Pallas kernels for 0% -> 65%
where the time goes in v1:
time: 103 us; the launch traced here: 102 us
  Pallas kernels  67.8 us (66%)
  blocking collectives  14.6 us (14%)
  starting transfers between devices  10.6 us (10%)
  local copies, waits for them, and re-layouts  9.21 us (9%)
    pallas_call x1, Pallas kernels, per_device(): pl.pallas_call(functools.partial(inner_kernel, slots_yz), name='inner_dir...  44.8 us
    all_to_all x1, blocking collectives, per_device(): received_x = lax.all_to_all(sent_x, 'sx', 0, 0)  14.6 us
    pallas_call x1, Pallas kernels, per_device(): pl.pallas_call(functools.partial(last_kernel, slots_x), name='outer_direc...  11.7 us
    pallas_call x3, Pallas kernels, per_device(): pl.pallas_call(outer_kernel, name='outer_direction', out_shape=jax.ShapeD...  10.5 us
    ppermute x4, starting transfers between devices, per_device(): upper.append(lax.ppermute(piece, 'sx', route))  6.85 us
    unnamed x12, local copies, waits for them, and re-layouts  4.55 us
    all_to_all x1, starting transfers between devices, per_device(): received_yz = lax.all_to_all(sent_yz, 'sx', 0, 0)  3.72 us
    slice x1, local copies, waits for them, and re-layouts, per_device(): piece = eigvecs[q * part_modes:(q + 1) * part_modes, :, :, 0]  3.55 us
  transfers between devices with their start and end apart: 5, of which 0 were waited for; matrix products, arithmetic and copies ran while one was open for 3% of the time, Pallas kernels for 65%

profile of v1, /device:TPU:0, one launch (start us, length us, event | category | flops | bytes accessed | tf_op | source)
XLA Modules:
  0.0 102.4 jit_solution(580264364720100288)
XLA Ops:
  0.0 3.6 %fusion = (bf16[64,2,3,1,1024]{4,1,3,2,0:T(2,128)(2,1)S(1)}, bf16[64,2,3,1,1024]{4,1,3,2,0:T(2,128)(2,1)S(1)}, bf16[64,2,3,1,1024]{4,1,3,2,0:T(2,128)(2,1)S(1)}, bf16[64,2,3,1,1024]{4,1,3,2,0:T(2,128)(2,1)S(1)}) fusion(bf16[256,2,3,1,1024]{4,1,3,2,0:T(2,128)(2,1)} %param.3), kind=kLoop, calls=%fused_computation.4 | loop fusion | bytes 6291456 | tf_op jit(solution)/shard_map/slice | solution.py:345
  3.6 0.0 copy-start.3
  3.6 1.1 %copy.23 = bf16[64,2,3,1,1024]{4,0,1,2,3:T(8,128)(2,1)} copy(bf16[64,2,3,1,1024]{4,1,3,2,0:T(2,128)(2,1)S(1)} %get-tuple-element.12) | data formatting | bytes 1572864
  4.7 5.4 %collective-permute-start.2 = (bf16[3,2,64,1024]{3,2,1,0:T(8,128)(2,1)}, bf16[3,2,64,1024]{3,2,1,0:T(8,128)(2,1)}, u32[]{:S(2)}, u32[]{:S(2)}) collective-permute-start(bf16[3,2,64,1024]{3,2,1,0:T(8,128)(2,1)} %bitcast.18.refs_2_), channel_id=1, source_target_pairs={{0,15},{1,0},{2,1},{3,2},{4,3},{5,4},{6,5},{7,6},{8,7},{9,8},{10,9... | collective-permute-start | bytes 2359304 | tf_op jit(solution)/shard_map/ppermute | solution.py:348
  10.1 0.2 copy.24
  10.4 0.7 collective-permute-start.1
  11.1 0.2 copy.25
  11.3 0.1 collective-permute-start
  11.4 1.1 %copy.22 = bf16[64,2,3,1,1024]{4,0,1,2,3:T(8,128)(2,1)} copy(bf16[64,2,3,1,1024]{4,1,3,2,0:T(2,128)(2,1)S(1)} %get-tuple-element.11) | data formatting | bytes 1572864
  12.5 0.6 collective-permute-start.3
  13.1 0.0 copy-done.3
  13.1 0.1 reshape.24
  13.2 0.4 reshape.27.owner_ref
  13.6 0.0 copy-done.2
  13.6 44.8 %inner_directions.1 = (bf16[16,80,128]{2,1,0:T(8,128)(2,1)}, bf16[512,3072]{1,0:T(8,128)(2,1)}, f32[18,8,128]{2,1,0:T(8,128)S(1)}) custom-call(s32[3]{0:T(128)S(1)} %copy-done.2, s32[1]{0:T(128)} %bitcast.2.where_ref, s32[16,144,1]{2,1,0:T(8,128)S(1)} %reshape.27.owner_ref, bf16[3,2,64,1024]{3,2,1,0:T(8,128)(2,1)S(1)} %bitcast.24, ...), custom_call_target="tpu_custom_call" | custom-call | flops 6442450944 | bytes 12582912 | tf_op jit(solution)/shard_map/inner_directions/pallas_call | solution.py:353
  58.4 3.7 %all-to-all-start.1 = ((bf16[16,80,128]{2,1,0:T(8,128)(2,1)}), bf16[16,80,128]{2,1,0:T(8,128)(2,1)S(1)}, u32[]{:S(2)}, u32[]{:S(2)}) async-start(bf16[16,80,128]{2,1,0:T(8,128)(2,1)} %get-tuple-element.10), calls=%async_computation.1 | async-start | bytes 655360 | tf_op jit(solution)/shard_map/all_to_all | solution.py:373
  62.1 0.1 reshape.20
  62.3 0.1 reshape.21
  62.4 0.4 reshape.26.owner_ref
  62.8 0.0 collective-permute-done.2.vector_ref
  62.8 1.9 %copy-done = bf16[512,3072]{1,0:T(8,128)(2,1)S(1)} copy-done((bf16[512,3072]{1,0:T(8,128)(2,1)S(1)}, bf16[512,3072]{1,0:T(8,128)(2,1)}, u32[]{:S(2)}) %copy-start) | copy-done | bytes 3145752
  64.7 3.5 %outer_direction.5.refs_2_ = f32[2,64,256]{2,1,0:T(8,128)S(1)} custom-call(bf16[3,2,64,1024]{3,2,1,0:T(8,128)(2,1)} %collective-permute-done.2.vector_ref, f32[18,8,128]{2,1,0:T(8,128)S(1)} %get-tuple-element.8.links_ref.refs_4_, bf16[512,3072]{1,0:T(8,128)(2,1)S(1)} %copy-done), custom_call_target="tpu_custom_call" | custom-call | flops 402653184 | bytes 4194304 | tf_op jit(solution)/shard_map/outer_direction/pallas_call | solution.py:381
  68.1 0.0 copy-start.1
  68.2 0.0 collective-permute-done.1.vector_ref
  68.2 3.6 %outer_direction.4.refs_1_ = f32[2,64,256]{2,1,0:T(8,128)S(1)} custom-call(bf16[3,2,64,1024]{3,2,1,0:T(8,128)(2,1)} %collective-permute-done.1.vector_ref, f32[18,8,128]{2,1,0:T(8,128)S(1)} %get-tuple-element.8.links_ref.refs_4_, bf16[512,3072]{1,0:T(8,128)(2,1)S(1)} %copy-done), custom_call_target="tpu_custom_call" | custom-call | flops 402653184 | bytes 4194304 | tf_op jit(solution)/shard_map/outer_direction/pallas_call | solution.py:381
  71.8 0.0 collective-permute-done.vector_ref
  71.8 3.5 %outer_direction.3.refs_0_ = f32[2,64,256]{2,1,0:T(8,128)S(1)} custom-call(bf16[3,2,64,1024]{3,2,1,0:T(8,128)(2,1)} %collective-permute-done.vector_ref, f32[18,8,128]{2,1,0:T(8,128)S(1)} %get-tuple-element.8.links_ref.refs_4_, bf16[512,3072]{1,0:T(8,128)(2,1)S(1)} %copy-done), custom_call_target="tpu_custom_call" | custom-call | flops 402653184 | bytes 4194304 | tf_op jit(solution)/shard_map/outer_direction/pallas_call | solution.py:381
  75.3 0.0 collective-permute-done.3.refs_3_
  75.3 11.7 %outer_direction_tiles.1 = bf16[16,48,128]{2,1,0:T(8,128)(2,1)S(1)} custom-call(s32[16,160,1]{2,1,0:T(8,128)S(1)} %reshape.26.owner_ref, f32[2,64,256]{2,1,0:T(8,128)S(1)} %outer_direction.3.refs_0_, f32[2,64,256]{2,1,0:T(8,128)S(1)} %outer_direction.4.refs_1_, f32[2,64,256]{2,1,0:T(8,128)S(1)} %outer_direction.5.refs_2_, ...), custom_call_target="tpu_custom_call" | custom-call | flops 1610612736 | bytes 8388608 | tf_op jit(solution)/shard_map/outer_direction_tiles/pallas_call | solution.py:393
  87.0 0.0 all-to-all-done.1.yz_ref
  87.0 14.6 %all_to_all.10.x_ref = bf16[16,48,128]{2,1,0:T(8,128)(2,1)S(1)} all-to-all(bf16[16,48,128]{2,1,0:T(8,128)(2,1)S(1)} %outer_direction_tiles.1), channel_id=1, replica_groups=mesh['cfg'=2,'sx'=16] {'sx'}, dimensions={0} | all-to-all | bytes 393216 | tf_op jit(solution)/shard_map/all_to_all | solution.py:407
  101.6 0.8 sum_of_devices.1
  (6 shorter events, 0.0 us)
Async XLA Ops:
  3.6 9.5 %copy-start.3 = (s32[2080]{0:T(1024)S(1)}, s32[2080]{0:T(1024)}, u32[]{:S(2)}) copy-start(s32[2080]{0:T(1024)} %param.5) | copy-start | bytes 24964
  4.7 8.9 %copy-start.2 = (s32[3]{0:T(128)S(1)}, s32[3]{0:T(128)}, u32[]{:S(2)}) copy-start(s32[3]{0:T(128)} %seed_ref.1) | copy-start | bytes 40
  4.7 58.1 %collective-permute-start.2 = (bf16[3,2,64,1024]{3,2,1,0:T(8,128)(2,1)}, bf16[3,2,64,1024]{3,2,1,0:T(8,128)(2,1)}, u32[]{:S(2)}, u32[]{:S(2)}) collective-permute-start(bf16[3,2,64,1024]{3,2,1,0:T(8,128)(2,1)} %bitcast.18.refs_2_), channel_id=1, source_target_pairs={{0,15},{1,0},{2,1},{3,2},{4,3},{5,4},{6,5},{7,6},{8,7},{9,8},{10,9... | collective-permute-start | bytes 2359304 | tf_op jit(solution)/shard_map/ppermute | solution.py:348
  10.4 57.8 %collective-permute-start.1 = (bf16[3,2,64,1024]{3,2,1,0:T(8,128)(2,1)S(1)}, bf16[3,2,64,1024]{3,2,1,0:T(8,128)(2,1)}, u32[]{:S(2)}, u32[]{:S(2)}) collective-permute-start(bf16[3,2,64,1024]{3,2,1,0:T(8,128)(2,1)S(1)} %bitcast.21), channel_id=1, source_target_pairs={{0,15},{1,0},{2,1},{3,2},{4,3},{5,4},{6,5},{7,6},{8,7},{9,8},{10,9... | collective-permute-start | bytes 2359304 | tf_op jit(solution)/shard_map/ppermute | solution.py:348
  11.3 60.5 %collective-permute-start = (bf16[3,2,64,1024]{3,2,1,0:T(8,128)(2,1)S(1)}, bf16[3,2,64,1024]{3,2,1,0:T(8,128)(2,1)}, u32[]{:S(2)}, u32[]{:S(2)}) collective-permute-start(bf16[3,2,64,1024]{3,2,1,0:T(8,128)(2,1)S(1)} %bitcast.23), channel_id=1, source_target_pairs={{0,15},{1,0},{2,1},{3,2},{4,3},{5,4},{6,5},{7,6},{8,7},{9,8},{10,9... | collective-permute-start | bytes 2359304 | tf_op jit(solution)/shard_map/ppermute | solution.py:348
  12.5 62.8 %collective-permute-start.3 = (bf16[3,2,64,1024]{3,2,1,0:T(8,128)(2,1)}, bf16[3,2,64,1024]{3,2,1,0:T(8,128)(2,1)}, u32[]{:S(2)}, u32[]{:S(2)}) collective-permute-start(bf16[3,2,64,1024]{3,2,1,0:T(8,128)(2,1)} %bitcast.17.refs_3_), channel_id=1, source_target_pairs={{0,15},{1,0},{2,1},{3,2},{4,3},{5,4},{6,5},{7,6},{8,7},{9,8},{10,9... | collective-permute-start | bytes 2359304 | tf_op jit(solution)/shard_map/ppermute | solution.py:348
  58.4 28.6 %all-to-all-start.1 = ((bf16[16,80,128]{2,1,0:T(8,128)(2,1)}), bf16[16,80,128]{2,1,0:T(8,128)(2,1)S(1)}, u32[]{:S(2)}, u32[]{:S(2)}) async-start(bf16[16,80,128]{2,1,0:T(8,128)(2,1)} %get-tuple-element.10), calls=%async_computation.1 | async-start | bytes 655360 | tf_op jit(solution)/shard_map/all_to_all | solution.py:373
  62.8 1.9 %copy-start = (bf16[512,3072]{1,0:T(8,128)(2,1)S(1)}, bf16[512,3072]{1,0:T(8,128)(2,1)}, u32[]{:S(2)}) copy-start(bf16[512,3072]{1,0:T(8,128)(2,1)} %get-tuple-element.9.left_hbm.refs_5_) | copy-start | bytes 9437188
  68.1 7.1 %copy-start.1 = (bf16[512,3072]{1,0:T(8,128)(2,1)S(1)}, bf16[512,3072]{1,0:T(8,128)(2,1)}, u32[]{:S(2)}) copy-start(bf16[512,3072]{1,0:T(8,128)(2,1)} %get-tuple-element.9.left_hbm.refs_5_) | copy-start | bytes 9437188
